TPU v7x, 128 devices: a whole 4x4x4 slice. The times are simulated.
128 devices in a mesh: ctx: 64 (over z, x, y_hi, core), grp: 2 (over y_lo).
Axes of the slice: x: 4, y: 4 (y_hi: 2, y_lo: 2; y = y_hi * 2 + y_lo), z: 4, core: 2. Of those that a mesh axis runs over, the one named last changes fastest.
Arguments:
- queries: bfloat16 [16384, 1024], P('ctx', 'grp'), parts along dimension 1, may hold values from -5.5 to 5.5
- key_rows: bfloat16 [16384, 256], P('ctx', 'grp'), parts along dimension 1, may hold values from -5.5 to 5.5
- value_rows: bfloat16 [16384, 256], P('ctx', 'grp'), parts along dimension 1, may hold values from -6 to 6
Outputs:
- attended: bfloat16 [16384, 1024], P('ctx', 'grp'), parts along dimension 1
There are 2 independent parts, one for each index of `grp`. A program takes and returns all parts, laid end to end along the dimension named above; each array names one. Nothing has to cross between parts.
All inputs are finite; a program needn't handle non-finite values.
Results may differ from a plain program's by a relative error of at most 0.0029.
Values may be sent and summed in bfloat16 or wider, within the bound.
A program may use at most 192 MiB of HBM per device.

v0:
```python
import jax
import jax.numpy as jnp
from jax import lax
from jax.sharding import PartitionSpec as P

masked_fill = -1e30


def make_advance(grouped, query_pos, key_piece, value_piece, score_scale):

    def advance(state):
        run_max, run_sum, run_acc = state
        scores = (
            jnp.einsum("rhd,kd->rhk", grouped, key_piece, preferred_element_type=jnp.float32)
            * score_scale
        )
        key_pos = jnp.arange(key_piece.shape[0], dtype=jnp.int32)
        visible = key_pos[None, None, :] <= query_pos[:, None, None]
        scores = jnp.where(visible, scores, masked_fill)
        new_max = jnp.maximum(run_max, jnp.max(scores, axis=-1))
        weights = jnp.where(visible, jnp.exp(scores - new_max[..., None]), jnp.float32(0.0))
        new_sum = jnp.sum(weights, axis=-1)
        product = jnp.einsum(
            "rhk,kd->rhd",
            weights.astype(jnp.bfloat16),
            value_piece,
            preferred_element_type=jnp.float32,
        )
        return (new_max, new_sum, product)

    return advance


def passing(state):
    return state


def attend(segments, key_rows, value_rows):
    head_size = key_rows.shape[1]
    score_scale = 1.0 / head_size**0.5
    groups = []
    latests = []
    initial = []
    for query_block, query_pos in segments:
        row_count = query_block.shape[0]
        head_count = query_block.shape[1] // head_size
        groups.append(query_block.reshape(row_count, head_count, head_size))
        latests.append(jnp.max(query_pos))
        initial.append(
            (
                jnp.full((row_count, head_count), masked_fill, jnp.float32),
                jnp.zeros((row_count, head_count), jnp.float32),
                jnp.zeros((row_count, head_count, head_size), jnp.float32),
            )
        )
    key_piece = lax.all_gather(key_rows, "ctx", axis=0, tiled=True)
    value_piece = lax.all_gather(value_rows, "ctx", axis=0, tiled=True)
    number = 0
    advance = make_advance(groups[number], segments[number][1], key_piece, value_piece, score_scale)
    updated = [lax.cond(jnp.int32(0) > latests[number], passing, advance, tuple(initial)[number])]
    final = tuple(updated)
    number = 0
    final_max, final_sum, final_acc = final[number]
    row_count = final_acc.shape[0]
    outputs = [
        (final_acc / final_sum[..., None])
        .astype(jnp.bfloat16)
        .reshape(row_count, final_acc.shape[1] * head_size)
    ]
    return outputs


def per_device(queries, key_rows, value_rows):
    row_count = queries.shape[0]
    my_index = lax.axis_index("ctx")
    own_pos = my_index * row_count + jnp.arange(row_count, dtype=jnp.int32)
    return attend([(queries, own_pos)], key_rows, value_rows)[0]


def solution(mesh):
    placed = (P("ctx", "grp"), P("ctx", "grp"), P("ctx", "grp"))
    return jax.shard_map(
        per_device, mesh=mesh, in_specs=placed, out_specs=P("ctx", "grp"), check_vma=False
    )
```

profile of v0, /device:TPU:70, one launch (start us, length us, event | category | flops | bytes accessed | tf_op | source)
XLA Modules:
  0.0 248.4 jit_solution(853547434786918359)
XLA Ops:
  6.5 0.0 all-gather.3.cloned.1.call-start
  6.5 0.7 all-gather.3.cloned.1.call-update
  7.3 0.0 all-gather.5.cloned.1.call-start
  7.3 0.7 all-gather.5.cloned.1.call-update
  8.0 0.6 fusion.15
  9.3 72.4 %all-gather.3.cloned.1.call-done = bf16[16384,128]{1,0:T(8,128)(2,1)} async-done(((bf16[256,128]{1,0:T(8,128)(2,1)}), bf16[16384,128]{1,0:T(8,128)(2,1)}) %all-gather.3.cloned.1.call-update) | async-done | bytes 4194320 | tf_op jit(solution)/shard_map/all_gather | solution.py:56
  81.8 72.0 %all-gather.5.cloned.1.call-done = bf16[16384,128]{1,0:T(8,128)(2,1)} async-done(((bf16[256,128]{1,0:T(8,128)(2,1)}), bf16[16384,128]{1,0:T(8,128)(2,1)}) %all-gather.5.cloned.1.call-update) | async-done | bytes 4194320 | tf_op jit(solution)/shard_map/all_gather | solution.py:57
  153.8 86.8 %conditional.1 = (f32[256,4]{0,1:T(4,128)S(1)}, f32[256,4,128]{2,0,1:T(8,128)S(1)}) conditional(s32[]{:T(128)} %convert_element_type.9, (s32[256]{0:T(256)S(1)}, bf16[256,512]{1,0:T(8,128)(2,1)}, bf16[16384,128]{1,0:T(8,128)(2,1)}, bf16[16384,128]{1,0:T(8,128)(2,1)}) %tuple.13, () %tuple.14), branch_computations={%region_1.4_spmd, %region_4.5_spmd} | conditional | flops 8812231680 | bytes 227304464 | solution.py:60
  153.8 4.5 %iota_compare_fusion = pred[256,16384]{1,0:T(8,128)(4,1)} fusion(s32[256]{0:T(256)S(1)} %get-tuple-element.14), kind=kLoop, calls=%fused_computation.7 | loop fusion | flops 4194304 | bytes 4195328 | tf_op jit(solution)/shard_map/cond/branch_0_fun/le | solution.py:18
  158.2 28.6 %fusion = (f32[256,4]{0,1:T(4,128)S(1)}, f32[256,4,16384]{2,0,1:T(8,128)}) fusion(pred[256,16384]{1,0:T(8,128)(4,1)} %iota_compare_fusion, bf16[16384,128]{1,0:T(8,128)(2,1)} %get-tuple-element.16, bf16[256,512]{1,0:T(8,128)(2,1)} %get-tuple-element.23), kind=kOutput, calls=%fused_computation.2 | convolution fusion | flops 4345297920 | bytes 75763712 | tf_op jit(solution)/shard_map/cond/branch_0_fun/rhd,kd->rhk/dot_general | solution.py:14
  186.8 30.5 %fusion.3 = f32[256,4,128]{2,0,1:T(8,128)S(1)} fusion(f32[256,4,16384]{2,0,1:T(8,128)} %get-tuple-element.25, f32[256,4]{0,1:T(4,128)S(1)} %broadcast_maximum_fusion, pred[256,16384]{1,0:T(8,128)(4,1)} %iota_compare_fusion, bf16[16384,128]{1,0:T(8,128)(2,1)} %get-tuple-element.17), kind=kOutput, calls=%fused_computation.5 | convolution fusion | flops 4378853376 | bytes 76025856 | tf_op jit(solution)/shard_map/cond/branch_0_fun/rhk,kd->rhd/dot_general | solution.py:23
  217.4 23.0 %fusion.2 = f32[256,4]{0,1:T(4,128)S(1)} fusion(f32[256,4,16384]{2,0,1:T(8,128)} %get-tuple-element.25, f32[256,4]{0,1:T(4,128)S(1)} %broadcast_maximum_fusion, pred[256,16384]{1,0:T(8,128)(4,1)} %iota_compare_fusion), kind=kLoop, calls=%fused_computation.4 | loop fusion | flops 83885056 | bytes 71311360 | tf_op jit(solution)/shard_map/cond/branch_0_fun/reduce_sum | solution.py:22
  240.6 0.9 copy_bitcast_fusion
  (2 shorter events, 0.0 us)
Async XLA Ops:
  6.5 75.2 %all-gather.3.cloned.1.call-start = ((), (), s32[]{:S(2)}) async-start(), calls=%async_computation | async-start | bytes 4259840 | tf_op jit(solution)/shard_map/all_gather | solution.py:56
  7.3 146.5 %all-gather.5.cloned.1.call-start = ((), (), s32[]{:S(2)}) async-start(), calls=%async_computation.1 | async-start | bytes 4259840 | tf_op jit(solution)/shard_map/all_gather | solution.py:57
Sparse Core Ops, SparseCore 0:
  10.5 71.2 all-gather.2
  84.9 68.8 all-gather.4
where the time goes:
time: 253 us; the launch traced here: 248 us
  waiting for transfers between devices  146 us (58%)
  matrix products  59.2 us (23%)
  other arithmetic  29 us (11%)
  between operations  14.1 us (6%)
    all_gather x1, waiting for transfers between devices, attend(): key_piece = lax.all_gather(key_rows, 'ctx', axis=0, tiled=True)  72.4 us
    all_gather x1, waiting for transfers between devices, attend(): value_piece = lax.all_gather(value_rows, 'ctx', axis=0, tiled=True)  72 us
    dot_general x1, matrix products, advance(): jnp.einsum('rhk,kd->rhd', weights.astype(jnp.bfloat16), value_piece, pref...  30.5 us
    dot_general x1, matrix products, advance(): jnp.einsum('rhd,kd->rhk', grouped, key_piece, preferred_element_type=jnp....  28.6 us
    reduce_sum x1, other arithmetic, advance(): new_sum = jnp.sum(weights, axis=-1)  23 us
  transfers between devices with their start and end apart: 2, of which 2 were waited for; matrix products, arithmetic and copies ran while one was open for 0% of the time, Pallas kernels for 0%

commit v1 on v0

v1 whole, which is shorter than its diff:
```python
import math

import jax
import jax.numpy as jnp
from jax import lax
from jax.experimental import pallas as pl
from jax.experimental.pallas import tpu as pltpu
from jax.sharding import PartitionSpec as P

MESH = pl.DeviceIdType.MESH
F32 = jnp.float32
BF16 = jnp.bfloat16
LOW = -1e30
ROWS = 256
HD = 128
HEADS = 4
COLS = ROWS * HEADS
PLACES = 16
EARLY = 3


def dot(a, b):
    return lax.dot_general(a, b, (((1,), (0,)), ((), ())), preferred_element_type=F32)


def kernel(
    q_ref, k_ref, v_ref, out_ref,
    blocks, q_other, q_t, m_ref, l_ref, acc, s_a, s_b, p_a, p_b, al_a, al_b,
    part_o, part_ml, got_o, got_ml,
    to_sem, from_sem, pass_sem, passed_sem, q_sems, part_sems, ml_sems,
):
    ctx = lax.axis_index("ctx")
    grp = lax.axis_index("grp")
    place = ctx // 4
    y = (ctx // 2) % 2
    core = ctx % 2
    sibling = (ctx + 1 - 2 * core, grp)
    partner = (ctx + 2 - 4 * y, grp)
    pairs = place // 2
    odd = place % 2

    def at(other_place):
        return (other_place * 4 + y * 2 + core, grp)

    barrier = pltpu.get_barrier_semaphore()
    pl.semaphore_signal(barrier, inc=1, device_id=sibling, device_id_type=MESH)
    pl.semaphore_signal(barrier, inc=1, device_id=partner, device_id_type=MESH)

    def greet(i, _):
        pl.semaphore_signal(barrier, inc=1, device_id=at(i), device_id_type=MESH)
        return 0

    lax.fori_loop(0, place, greet, 0)

    mine = place * 2 + core
    blocks[mine, :ROWS] = k_ref[...]
    v_t = jnp.transpose(v_ref[...].astype(F32)).astype(BF16)
    blocks[mine, ROWS : ROWS + HD] = v_t[:, :HD]
    blocks[mine, ROWS + HD :] = v_t[:, HD:]

    pl.semaphore_wait(barrier, 17 - place)

    def copy(src, dst, send, recv, device):
        return pltpu.make_async_remote_copy(
            src_ref=src, dst_ref=dst, send_sem=send, recv_sem=recv,
            device_id=device, device_id_type=MESH,
        )

    def block_to(other_place):
        return copy(
            blocks.at[mine], blocks.at[mine], to_sem.at[other_place], from_sem.at[place], at(other_place)
        )

    def block_from(other_place):
        here = other_place * 2 + core
        return copy(
            blocks.at[here], blocks.at[here], to_sem.at[other_place], from_sem.at[other_place], at(other_place)
        )

    def block_pass(other_place):
        here = other_place * 2 + core
        return copy(
            blocks.at[here], blocks.at[here], pass_sem.at[other_place], passed_sem.at[other_place], sibling
        )

    def block_passed(other_place):
        here = other_place * 2 + 1 - core
        return copy(
            blocks.at[here], blocks.at[here], pass_sem.at[other_place], passed_sem.at[other_place], sibling
        )

    q_copy = copy(q_ref, q_other, q_sems.at[0], q_sems.at[1], partner)
    block_pass(place).start()
    q_copy.start()

    def send(i, _):
        block_to(i).start()
        return 0

    lax.fori_loop(place + 1, PLACES, send, 0)

    scale = math.log2(math.e) / math.sqrt(HD)

    def ready_queries(ref, s):
        for h in range(HEADS):
            full = jnp.transpose(ref[:, h * HD : (h + 1) * HD].astype(F32)) * scale
            hi = full.astype(BF16)
            q_t[s, :HD, h * ROWS : (h + 1) * ROWS] = hi
            q_t[s, HD:, h * ROWS : (h + 1) * ROWS] = (full - hi.astype(F32)).astype(BF16)

    m_ref[...] = jnp.full(m_ref.shape, LOW, F32)
    l_ref[...] = jnp.zeros(l_ref.shape, F32)
    acc[...] = jnp.zeros(acc.shape, F32)
    ready_queries(q_ref, 0)

    s_refs, p_refs, al_refs = (s_a, s_b), (p_a, p_b), (al_a, al_b)

    def keys(first, count):
        k = jnp.concatenate([blocks[first + i, :ROWS] for i in range(count)], 0)
        return jnp.concatenate([k, k], 1)

    def values(first, count):
        tiles = []
        for i in range(count):
            tiles.append(blocks[first + i, ROWS : ROWS + HD])
            tiles.append(blocks[first + i, ROWS + HD :])
        return jnp.concatenate(tiles, 1)

    def cols(h):
        return slice(h * ROWS, (h + 1) * ROWS)

    def scores(s, k, h, slot):
        s_refs[slot][: k.shape[0]] = dot(k, q_t[s, :, cols(h)])

    def weigh(s, h, slot, count, masked):
        n = count * ROWS
        score = s_refs[slot][:n]
        if masked:
            key_at = lax.broadcasted_iota(jnp.int32, (n, ROWS), 0)
            query_at = lax.broadcasted_iota(jnp.int32, (n, ROWS), 1) + core * ROWS
            score = jnp.where(key_at <= query_at, score, LOW)
        old = m_ref[s, :, cols(h)]
        top = jnp.max(score.reshape(n // 8, 8, ROWS), axis=0)
        new = jnp.maximum(old, jnp.max(top, axis=0, keepdims=True))
        w = jnp.exp2(score - new[:1])
        alpha = jnp.exp2(old - new)
        l_ref[s, :, cols(h)] = l_ref[s, :, cols(h)] * alpha + jnp.sum(w.reshape(n // 8, 8, ROWS), axis=0)
        p_refs[slot][:n] = w.astype(BF16)
        al_refs[slot][...] = alpha
        m_ref[s, :, cols(h)] = new

    def gather(s, v, h, slot):
        n = v.shape[1]
        acc[s, :, cols(h)] = acc[s, :, cols(h)] * al_refs[slot][:1] + dot(v, p_refs[slot][:n])

    def one_place(s, other_place, masked):
        first = other_place * 2
        k, v = keys(first, 2), values(first, 2)
        scores(s, k, 0, 0)
        for h in range(HEADS):
            if h + 1 < HEADS:
                scores(s, k, h + 1, (h + 1) % 2)
            if h > 0:
                gather(s, v, h - 1, (h - 1) % 2)
            weigh(s, h, h % 2, 2, masked)
        gather(s, v, HEADS - 1, (HEADS - 1) % 2)

    def first_block(t):
        return 4 * (pairs - 1 - t)

    def arrive(t):
        @pl.when(t < pairs)
        def _():
            for other_place in (2 * (pairs - 1 - t) + 1, 2 * (pairs - 1 - t)):
                block_from(other_place).wait_recv()
                block_pass(other_place).start()

    def complete(t):
        @pl.when(t < pairs)
        def _():
            for other_place in (2 * (pairs - 1 - t) + 1, 2 * (pairs - 1 - t)):
                block_passed(other_place).wait_recv()

    def phase(s, lo, hi, wait_from):
        @pl.when(lo < hi)
        def _():
            scores(s, keys(first_block(lo), 4), 0, 0)
            p_b[...] = jnp.zeros(p_b.shape, BF16)
            al_b[...] = jnp.ones(al_b.shape, F32)

            def item(t, _):
                if wait_from is not None:
                    @pl.when(t >= wait_from)
                    def _():
                        arrive(t + 2)
                        complete(t + 1)
                k, v = keys(first_block(t), 4), values(first_block(t), 4)
                k_next = keys(first_block(jnp.minimum(t + 1, hi - 1)), 4)
                v_last = values(first_block(jnp.maximum(t - 1, lo)), 4)
                for h in range(HEADS):
                    if h + 1 < HEADS:
                        scores(s, k, h + 1, (h + 1) % 2)
                    else:
                        scores(s, k_next, 0, 0)
                    if h > 0:
                        gather(s, v, h - 1, (h - 1) % 2)
                    else:
                        gather(s, v_last, HEADS - 1, 1)
                    weigh(s, h, h % 2, 4, False)
                return 0

            lax.fori_loop(lo, hi, item, 0)
            gather(s, values(first_block(hi - 1), 4), HEADS - 1, 1)

    block_passed(place).wait_recv()
    one_place(0, place, True)

    @pl.when(odd == 1)
    def _():
        block_from(place - 1).wait_recv()
        block_pass(place - 1).start()

    arrive(0)

    @pl.when(odd == 1)
    def _():
        block_passed(place - 1).wait_recv()
        one_place(0, place - 1, False)

    arrive(1)
    complete(0)
    early = jnp.minimum(pairs, EARLY)
    phase(0, 0, early, 0)

    q_copy.wait_recv()
    ready_queries(q_other, 1)

    @pl.when(y == 0)
    def _():
        one_place(1, place, False)

    @pl.when(odd == 1)
    def _():
        one_place(1, place - 1, False)

    phase(1, 0, pairs, EARLY)
    l_other = jnp.sum(l_ref[1], axis=0, keepdims=True)
    part_o[...] = (acc[1] / jnp.where(l_other > 0, l_other, 1.0)).astype(BF16)
    part_ml[0:1] = m_ref[1, 0:1]
    part_ml[1:2] = l_other
    part_ml[2:] = jnp.zeros((6, COLS), F32)
    o_copy = copy(part_o, got_o, part_sems.at[0], part_sems.at[1], partner)
    ml_copy = copy(part_ml, got_ml, ml_sems.at[0], ml_sems.at[1], partner)
    o_copy.start()
    ml_copy.start()

    phase(0, early, pairs, None)

    o_copy.wait_recv()
    ml_copy.wait_recv()
    m_own, m_got = m_ref[0, 0:1], got_ml[0:1]
    top = jnp.maximum(m_own, m_got)
    a_own = jnp.exp2(m_own - top)
    a_got = jnp.exp2(m_got - top) * got_ml[1:2]
    total = jnp.sum(l_ref[0], axis=0, keepdims=True) * a_own + a_got
    f_own, f_got = a_own / total, a_got / total
    for h in range(HEADS):
        o = acc[0, :, cols(h)] * f_own[:, cols(h)] + got_o[:, cols(h)].astype(F32) * f_got[:, cols(h)]
        out_ref[:, h * HD : (h + 1) * HD] = jnp.transpose(o).astype(BF16)

    o_copy.wait_send()
    ml_copy.wait_send()
    q_copy.wait_send()

    def sent(i, _):
        block_to(i).wait_send()
        return 0

    lax.fori_loop(place + 1, PLACES, sent, 0)

    def passed_on(i, _):
        block_pass(i).wait_send()
        return 0

    lax.fori_loop(0, place + 1, passed_on, 0)


def per_device(queries, key_rows, value_rows):
    vmem = pl.BlockSpec(memory_space=pltpu.VMEM)
    return pl.pallas_call(
        kernel,
        out_shape=jax.ShapeDtypeStruct((ROWS, HEADS * HD), BF16),
        in_specs=[vmem] * 3,
        out_specs=vmem,
        scratch_shapes=[
            pltpu.VMEM((PLACES * 2, 2 * ROWS, HD), BF16),
            pltpu.VMEM((ROWS, HEADS * HD), BF16),
            pltpu.VMEM((2, 2 * HD, COLS), BF16),
            pltpu.VMEM((2, 8, COLS), F32),
            pltpu.VMEM((2, 8, COLS), F32),
            pltpu.VMEM((2, HD, COLS), F32),
            pltpu.VMEM((4 * ROWS, ROWS), F32),
            pltpu.VMEM((4 * ROWS, ROWS), F32),
            pltpu.VMEM((4 * ROWS, ROWS), BF16),
            pltpu.VMEM((4 * ROWS, ROWS), BF16),
            pltpu.VMEM((8, ROWS), F32),
            pltpu.VMEM((8, ROWS), F32),
            pltpu.VMEM((HD, COLS), BF16),
            pltpu.VMEM((8, COLS), F32),
            pltpu.VMEM((HD, COLS), BF16),
            pltpu.VMEM((8, COLS), F32),
            pltpu.SemaphoreType.DMA((PLACES,)),
            pltpu.SemaphoreType.DMA((PLACES,)),
            pltpu.SemaphoreType.DMA((PLACES,)),
            pltpu.SemaphoreType.DMA((PLACES,)),
            pltpu.SemaphoreType.DMA((2,)),
            pltpu.SemaphoreType.DMA((2,)),
            pltpu.SemaphoreType.DMA((2,)),
        ],
        compiler_params=pltpu.CompilerParams(
            collective_id=0, has_side_effects=True, vmem_limit_bytes=48 << 20
        ),
        name="attend",
    )(queries, key_rows, value_rows)


def solution(mesh):
    placed = (P("ctx", "grp"), P("ctx", "grp"), P("ctx", "grp"))
    return jax.shard_map(
        per_device, mesh=mesh, in_specs=placed, out_specs=P("ctx", "grp"), check_vma=False
    )
```

time: 253 us -> 55.8 us (0.22)
  the two profiles are of different devices: /device:TPU:70 before, /device:TPU:96 now
where the time goes in v1:
time: 55.8 us; the launch traced here: 55.6 us
  Pallas kernels  52.2 us (94%)
  local copies, waits for them, and re-layouts  3.33 us (6%)
    pallas_call x1, Pallas kernels, per_device(): pl.pallas_call(kernel, out_shape=jax.ShapeDtypeStruct((ROWS, HEADS * HD),...  52.2 us
    unnamed x7, local copies, waits for them, and re-layouts  3.33 us

profile of v1, /device:TPU:96, one launch (start us, length us, event | category | flops | bytes accessed | tf_op | source)
XLA Modules:
  0.0 55.6 jit_solution(16493078025298152654)
XLA Ops:
  0.0 0.0 copy-start
  0.0 0.9 %copy-done = bf16[256,512]{1,0:T(8,128)(2,1)S(1)} copy-done((bf16[256,512]{1,0:T(8,128)(2,1)S(1)}, bf16[256,512]{1,0:T(8,128)(2,1)}, u32[]{:S(2)}) %copy-start) | copy-done | bytes 262168
  1.0 0.0 copy-start.1
  1.0 0.8 %copy-done.1 = bf16[256,128]{1,0:T(8,128)(2,1)S(1)} copy-done((bf16[256,128]{1,0:T(8,128)(2,1)S(1)}, bf16[256,128]{1,0:T(8,128)(2,1)}, u32[]{:S(2)}) %copy-start.1) | copy-done | bytes 65560
  1.8 0.0 copy-start.2
  1.8 0.8 %copy-done.2 = bf16[256,128]{1,0:T(8,128)(2,1)S(1)} copy-done((bf16[256,128]{1,0:T(8,128)(2,1)S(1)}, bf16[256,128]{1,0:T(8,128)(2,1)}, u32[]{:S(2)}) %copy-start.2) | copy-done | bytes 65560
  2.6 52.2 %attend.1 = bf16[256,512]{1,0:T(8,128)(2,1)S(1)} custom-call(bf16[256,512]{1,0:T(8,128)(2,1)S(1)} %copy-done, bf16[256,128]{1,0:T(8,128)(2,1)S(1)} %copy-done.1, bf16[256,128]{1,0:T(8,128)(2,1)S(1)} %copy-done.2), custom_call_target="tpu_custom_call" | custom-call | tf_op jit(solution)/shard_map/attend/pallas_call | solution.py:290
  54.9 0.7 %copy.5 = bf16[256,512]{1,0:T(8,128)(2,1)} copy(bf16[256,512]{1,0:T(8,128)(2,1)S(1)} %attend.1) | data formatting | bytes 524288
Async XLA Ops:
  0.0 0.9 %copy-start = (bf16[256,512]{1,0:T(8,128)(2,1)S(1)}, bf16[256,512]{1,0:T(8,128)(2,1)}, u32[]{:S(2)}) copy-start(bf16[256,512]{1,0:T(8,128)(2,1)} %q_ref.1) | copy-start | bytes 786436
  1.0 0.8 %copy-start.1 = (bf16[256,128]{1,0:T(8,128)(2,1)S(1)}, bf16[256,128]{1,0:T(8,128)(2,1)}, u32[]{:S(2)}) copy-start(bf16[256,128]{1,0:T(8,128)(2,1)} %k_ref.1) | copy-start | bytes 196612
  1.8 0.8 %copy-start.2 = (bf16[256,128]{1,0:T(8,128)(2,1)S(1)}, bf16[256,128]{1,0:T(8,128)(2,1)}, u32[]{:S(2)}) copy-start(bf16[256,128]{1,0:T(8,128)(2,1)} %v_ref.1) | copy-start | bytes 196612

commit v2 on v1

--- a/solution.py
+++ b/solution.py
@@ -27,7 +27,7 @@
     q_ref, k_ref, v_ref, out_ref,
     blocks, q_other, q_t, m_ref, l_ref, acc, s_a, s_b, p_a, p_b, al_a, al_b,
     part_o, part_ml, got_o, got_ml,
-    to_sem, from_sem, pass_sem, passed_sem, q_sems, part_sems, ml_sems,
+    x_sem, z_sem, from_sem, pass_sem, passed_sem, q_sems, part_sems, ml_sems,
 ):
     ctx = lax.axis_index("ctx")
     grp = lax.axis_index("grp")
@@ -38,19 +38,32 @@
     partner = (ctx + 2 - 4 * y, grp)
     pairs = place // 2
     odd = place % 2
+    z, x = place // 4, place % 4
+    along_x = core == 0
 
     def at(other_place):
         return (other_place * 4 + y * 2 + core, grp)
+
+    def mates(step):
+        for dx in (1, 3, 2):
+            mate = (x + dx) % 4
+            through = jnp.logical_or(jnp.logical_and(along_x, z < 3), jnp.logical_and(core == 1, z > 0))
+            step(mate, jnp.logical_or(through, mate > x), jnp.logical_or(through, mate < x))
 
     barrier = pltpu.get_barrier_semaphore()
     pl.semaphore_signal(barrier, inc=1, device_id=sibling, device_id_type=MESH)
     pl.semaphore_signal(barrier, inc=1, device_id=partner, device_id_type=MESH)
 
-    def greet(i, _):
-        pl.semaphore_signal(barrier, inc=1, device_id=at(i), device_id_type=MESH)
-        return 0
-
-    lax.fori_loop(0, place, greet, 0)
+    def greet(mate, _, hears):
+        @pl.when(hears)
+        def _():
+            pl.semaphore_signal(barrier, inc=1, device_id=at(z * 4 + mate), device_id_type=MESH)
+
+    mates(greet)
+    for below in range(3):
+        @pl.when(below < z)
+        def _(below=below):
+            pl.semaphore_signal(barrier, inc=1, device_id=at(below * 4 + x), device_id_type=MESH)
 
     mine = place * 2 + core
     blocks[mine, :ROWS] = k_ref[...]
@@ -58,7 +71,8 @@
     blocks[mine, ROWS : ROWS + HD] = v_t[:, :HD]
     blocks[mine, ROWS + HD :] = v_t[:, HD:]
 
-    pl.semaphore_wait(barrier, 17 - place)
+    through = jnp.where(along_x, z < 3, z > 0)
+    pl.semaphore_wait(barrier, 5 - z + jnp.where(through, 3, 3 - x))
 
     def copy(src, dst, send, recv, device):
         return pltpu.make_async_remote_copy(
@@ -66,15 +80,40 @@
             device_id=device, device_id_type=MESH,
         )
 
-    def block_to(other_place):
+    def along_x_copy(plane, mate):
+        here = (plane * 4 + x) * 2 + core
         return copy(
-            blocks.at[mine], blocks.at[mine], to_sem.at[other_place], from_sem.at[place], at(other_place)
-        )
+            blocks.at[here], blocks.at[here], x_sem.at[plane, mate], from_sem.at[plane * 4 + x], at(z * 4 + mate)
+        )
+
+    def along_z_copy(column, above):
+        here = (z * 4 + column) * 2 + core
+        return copy(
+            blocks.at[here], blocks.at[here], z_sem.at[column, above], from_sem.at[z * 4 + column], at(above * 4 + x)
+        )
+
+    def up(column, step):
+        for dz in (1, 2, 3):
+            @pl.when(z + dz < 4)
+            def _(dz=dz):
+                step(along_z_copy(column, z + dz))
+
+    def across(plane, step):
+        for dx in (1, 3, 2):
+            step(along_x_copy(plane, (x + dx) % 4))
+
+    def own_across(step):
+        def one(mate, sends, _):
+            @pl.when(jnp.logical_or(jnp.logical_and(along_x, z < 3), mate > x))
+            def _():
+                step(along_x_copy(z, mate))
+
+        mates(one)
 
     def block_from(other_place):
         here = other_place * 2 + core
         return copy(
-            blocks.at[here], blocks.at[here], to_sem.at[other_place], from_sem.at[other_place], at(other_place)
+            blocks.at[here], blocks.at[here], x_sem.at[0, 0], from_sem.at[other_place], sibling
         )
 
     def block_pass(other_place):
@@ -93,11 +132,18 @@
     block_pass(place).start()
     q_copy.start()
 
-    def send(i, _):
-        block_to(i).start()
-        return 0
-
-    lax.fori_loop(place + 1, PLACES, send, 0)
+    def start(c):
+        c.start()
+
+    @pl.when(core == 0)
+    def _():
+        own_across(start)
+        up(x, start)
+
+    @pl.when(core == 1)
+    def _():
+        up(x, start)
+        own_across(start)
 
     scale = math.log2(math.e) / math.sqrt(HD)
 
@@ -168,12 +214,49 @@
     def first_block(t):
         return 4 * (pairs - 1 - t)
 
+    def take(other_place):
+        relayed = jnp.where(along_x, other_place // 4 == z, other_place % 4 == x)
+
+        @pl.when(jnp.logical_not(relayed))
+        def _():
+            block_from(other_place).wait_recv()
+            block_pass(other_place).start()
+
     def arrive(t):
         @pl.when(t < pairs)
         def _():
-            for other_place in (2 * (pairs - 1 - t) + 1, 2 * (pairs - 1 - t)):
-                block_from(other_place).wait_recv()
-                block_pass(other_place).start()
+            take(2 * (pairs - 1 - t) + 1)
+            take(2 * (pairs - 1 - t))
+
+    def relay(step_up, step_across):
+        @pl.when(core == 0)
+        def _():
+            def one(mate, _, hears):
+                @pl.when(hears)
+                def _():
+                    step_up(mate)
+
+            mates(one)
+
+        @pl.when(core == 1)
+        def _():
+            for dz in (1, 2, 3):
+                @pl.when(z >= dz)
+                def _(dz=dz):
+                    step_across(z - dz)
+
+    def relay_up(mate):
+        block_from(z * 4 + mate).wait_recv()
+        up(mate, start)
+
+        @pl.when(mate < x)
+        def _():
+            block_pass(z * 4 + mate).start()
+
+    def relay_across(plane):
+        block_from(plane * 4 + x).wait_recv()
+        across(plane, start)
+        block_pass(plane * 4 + x).start()
 
     def complete(t):
         @pl.when(t < pairs)
@@ -214,11 +297,11 @@
 
     block_passed(place).wait_recv()
     one_place(0, place, True)
+    relay(relay_up, relay_across)
 
     @pl.when(odd == 1)
     def _():
-        block_from(place - 1).wait_recv()
-        block_pass(place - 1).start()
+        take(place - 1)
 
     arrive(0)
 
@@ -272,11 +355,12 @@
     ml_copy.wait_send()
     q_copy.wait_send()
 
-    def sent(i, _):
-        block_to(i).wait_send()
-        return 0
-
-    lax.fori_loop(place + 1, PLACES, sent, 0)
+    def gone(c):
+        c.wait_send()
+
+    own_across(gone)
+    up(x, gone)
+    relay(lambda mate: up(mate, gone), lambda plane: across(plane, gone))
 
     def passed_on(i, _):
         block_pass(i).wait_send()
@@ -309,7 +393,8 @@
             pltpu.VMEM((8, COLS), F32),
             pltpu.VMEM((HD, COLS), BF16),
             pltpu.VMEM((8, COLS), F32),
-            pltpu.SemaphoreType.DMA((PLACES,)),
+            pltpu.SemaphoreType.DMA((4, 4)),
+            pltpu.SemaphoreType.DMA((4, 4)),
             pltpu.SemaphoreType.DMA((PLACES,)),
             pltpu.SemaphoreType.DMA((PLACES,)),
             pltpu.SemaphoreType.DMA((PLACES,)),

time: 55.8 us -> 47.4 us (0.85)
  the two profiles are of different devices: /device:TPU:96 before, /device:TPU:70 now
where the time goes in v2:
time: 47.4 us; the launch traced here: 46.5 us
  Pallas kernels  43.1 us (91%)
  local copies, waits for them, and re-layouts  3.33 us (7%)
    pallas_call x1, Pallas kernels, per_device(): pl.pallas_call(kernel, out_shape=jax.ShapeDtypeStruct((ROWS, HEADS * HD),...  43.1 us
    unnamed x7, local copies, waits for them, and re-layouts  3.33 us

profile of v2, /device:TPU:70, one launch (start us, length us, event | category | flops | bytes accessed | tf_op | source)
XLA Modules:
  0.0 46.5 jit_solution(7478300006231610429)
XLA Ops:
  0.0 0.0 copy-start
  0.0 0.9 %copy-done = bf16[256,512]{1,0:T(8,128)(2,1)S(1)} copy-done((bf16[256,512]{1,0:T(8,128)(2,1)S(1)}, bf16[256,512]{1,0:T(8,128)(2,1)}, u32[]{:S(2)}) %copy-start) | copy-done | bytes 262168
  1.0 0.0 copy-start.1
  1.0 0.8 %copy-done.1 = bf16[256,128]{1,0:T(8,128)(2,1)S(1)} copy-done((bf16[256,128]{1,0:T(8,128)(2,1)S(1)}, bf16[256,128]{1,0:T(8,128)(2,1)}, u32[]{:S(2)}) %copy-start.1) | copy-done | bytes 65560
  1.8 0.0 copy-start.2
  1.8 0.8 %copy-done.2 = bf16[256,128]{1,0:T(8,128)(2,1)S(1)} copy-done((bf16[256,128]{1,0:T(8,128)(2,1)S(1)}, bf16[256,128]{1,0:T(8,128)(2,1)}, u32[]{:S(2)}) %copy-start.2) | copy-done | bytes 65560
  2.6 43.1 %attend.1 = bf16[256,512]{1,0:T(8,128)(2,1)S(1)} custom-call(bf16[256,512]{1,0:T(8,128)(2,1)S(1)} %copy-done, bf16[256,128]{1,0:T(8,128)(2,1)S(1)} %copy-done.1, bf16[256,128]{1,0:T(8,128)(2,1)S(1)} %copy-done.2), custom_call_target="tpu_custom_call" | custom-call | tf_op jit(solution)/shard_map/attend/pallas_call | solution.py:374
  45.8 0.7 %copy.5 = bf16[256,512]{1,0:T(8,128)(2,1)} copy(bf16[256,512]{1,0:T(8,128)(2,1)S(1)} %attend.1) | data formatting | bytes 524288
Async XLA Ops:
  0.0 0.9 %copy-start = (bf16[256,512]{1,0:T(8,128)(2,1)S(1)}, bf16[256,512]{1,0:T(8,128)(2,1)}, u32[]{:S(2)}) copy-start(bf16[256,512]{1,0:T(8,128)(2,1)} %q_ref.1) | copy-start | bytes 786436
  1.0 0.8 %copy-start.1 = (bf16[256,128]{1,0:T(8,128)(2,1)S(1)}, bf16[256,128]{1,0:T(8,128)(2,1)}, u32[]{:S(2)}) copy-start(bf16[256,128]{1,0:T(8,128)(2,1)} %k_ref.1) | copy-start | bytes 196612
  1.8 0.8 %copy-start.2 = (bf16[256,128]{1,0:T(8,128)(2,1)S(1)}, bf16[256,128]{1,0:T(8,128)(2,1)}, u32[]{:S(2)}) copy-start(bf16[256,128]{1,0:T(8,128)(2,1)} %v_ref.1) | copy-start | bytes 196612

commit v3 on v2

v3 whole, which is shorter than its diff:
```python
import math

import jax
import jax.numpy as jnp
from jax import lax
from jax.experimental import pallas as pl
from jax.experimental.pallas import tpu as pltpu
from jax.sharding import PartitionSpec as P

MESH = pl.DeviceIdType.MESH
F32 = jnp.float32
BF16 = jnp.bfloat16
LOW = -1e30
ROWS = 256
HD = 128
HEADS = 4
COLS = ROWS * HEADS
PLACES = 16
KEYS = 4 * ROWS
SETS = 4


def dot(a, b):
    return lax.dot_general(a, b, (((1,), (0,)), ((), ())), preferred_element_type=F32)


def kernel(
    q_in, k_in, v_in, out_ref,
    blocks, v_own, q_sets, q_t, ml_ref, acc, s_a, s_b, p_a, p_b, al_a, al_b,
    got_acc, got_ml, part_o, part_ml, got_o, got_oml,
    in_sem, x_sem, z_sem, from_sem, q_send, q_recv, acc_send, acc_recv, stat_send, stat_recv, o_sem, oml_sem,
):
    ctx = lax.axis_index("ctx")
    grp = lax.axis_index("grp")
    place = ctx // 4
    y = (ctx // 2) % 2
    core = ctx % 2
    sibling = (ctx + 1 - 2 * core, grp)
    partner = (ctx + 2 - 4 * y, grp)
    z, x = place // 4, place % 4
    along_x = core == 0

    def at(other_place):
        return (other_place * 4 + y * 2 + core, grp)

    through = jnp.where(along_x, z < 3, z > 0)

    def mates(step):
        for dx in (1, 3, 2):
            mate = (x + dx) % 4
            step(mate, jnp.logical_or(through, mate > x), jnp.logical_or(through, mate < x))

    k_get = pltpu.make_async_copy(k_in, blocks.at[place, pl.ds(0, ROWS)], in_sem.at[0])
    v_get = pltpu.make_async_copy(v_in, v_own, in_sem.at[1])
    q_get = pltpu.make_async_copy(q_in, q_sets.at[0], in_sem.at[2])
    v_get.start()
    k_get.start()
    q_get.start()

    barrier = pltpu.get_barrier_semaphore()
    pl.semaphore_signal(barrier, inc=1, device_id=sibling, device_id_type=MESH)
    pl.semaphore_signal(barrier, inc=1, device_id=partner, device_id_type=MESH)

    def greet(mate, _, hears):
        @pl.when(hears)
        def _():
            pl.semaphore_signal(barrier, inc=1, device_id=at(z * 4 + mate), device_id_type=MESH)

    mates(greet)
    for below in range(3):
        @pl.when(below < z)
        def _(below=below):
            pl.semaphore_signal(barrier, inc=1, device_id=at(below * 4 + x), device_id_type=MESH)

    ml_ref[:, :8] = jnp.full((SETS, 8, COLS), LOW, F32)
    ml_ref[:, 8:] = jnp.zeros((SETS, 8, COLS), F32)
    acc[...] = jnp.zeros(acc.shape, F32)

    v_get.wait()
    v_t = jnp.transpose(v_own[...].astype(F32)).astype(BF16)
    blocks[place, ROWS : ROWS + HD] = v_t[:, :HD]
    blocks[place, ROWS + HD :] = v_t[:, HD:]
    k_get.wait()
    q_get.wait()

    pl.semaphore_wait(barrier, 5 - z + jnp.where(through, 3, 3 - x))

    def copy(src, dst, send, recv, device):
        return pltpu.make_async_remote_copy(
            src_ref=src, dst_ref=dst, send_sem=send, recv_sem=recv,
            device_id=device, device_id_type=MESH,
        )

    def along_x_copy(plane, mate):
        here = plane * 4 + x
        return copy(blocks.at[here], blocks.at[here], x_sem.at[plane, mate], from_sem.at[here], at(z * 4 + mate))

    def along_z_copy(column, above):
        here = z * 4 + column
        return copy(blocks.at[here], blocks.at[here], z_sem.at[column, above], from_sem.at[here], at(above * 4 + x))

    def wait_block(here):
        copy(blocks.at[here], blocks.at[here], x_sem.at[0, 0], from_sem.at[here], sibling).wait_recv()

    def up(column, step):
        for dz in (1, 2, 3):
            @pl.when(z + dz < 4)
            def _(dz=dz):
                step(along_z_copy(column, z + dz))

    def across(plane, step):
        for dx in (1, 3, 2):
            step(along_x_copy(plane, (x + dx) % 4))

    def own_across(step):
        for dx in (1, 3, 2):
            mate = (x + dx) % 4

            @pl.when(jnp.logical_or(jnp.logical_and(along_x, z < 3), mate > x))
            def _(mate=mate):
                step(along_x_copy(z, mate))

    def start(c):
        c.start()

    def gone(c):
        c.wait_send()

    q_to_sibling = copy(q_sets.at[0], q_sets.at[1], q_send.at[0], q_recv.at[0], sibling)
    q_to_partner = copy(q_sets.at[0], q_sets.at[2], q_send.at[1], q_recv.at[1], partner)
    q_passed = copy(q_sets.at[2], q_sets.at[3], q_send.at[2], q_recv.at[2], sibling)

    q_to_partner.start()
    q_to_sibling.start()

    @pl.when(core == 0)
    def _():
        own_across(start)
        up(x, start)

    @pl.when(core == 1)
    def _():
        up(x, start)
        own_across(start)

    scale = math.log2(math.e) / math.sqrt(HD)

    def ready_queries(s):
        for h in range(HEADS):
            full = jnp.transpose(q_sets[s, :, h * HD : (h + 1) * HD].astype(F32)) * scale
            hi = full.astype(BF16)
            q_t[s, :HD, h * ROWS : (h + 1) * ROWS] = hi
            q_t[s, HD:, h * ROWS : (h + 1) * ROWS] = (full - hi.astype(F32)).astype(BF16)

    s_refs, p_refs, al_refs = (s_a, s_b), (p_a, p_b), (al_a, al_b)

    def keys(plane, count):
        k = jnp.concatenate([blocks[plane * 4 + i, :ROWS] for i in range(count)], 0)
        return jnp.concatenate([k, k], 1)

    def values(plane, count):
        tiles = []
        for i in range(count):
            tiles.append(blocks[plane * 4 + i, ROWS : ROWS + HD])
            tiles.append(blocks[plane * 4 + i, ROWS + HD :])
        return jnp.concatenate(tiles, 1)

    def cols(h):
        return slice(h * ROWS, (h + 1) * ROWS)

    def scores(s, k, h, slot):
        s_refs[slot][: k.shape[0]] = dot(k, q_t[s, :, cols(h)])

    def weigh(s, h, slot, n, visible):
        score = s_refs[slot][:n]
        if visible is not None:
            score = jnp.where(visible, score, LOW)
        old = ml_ref[s, :8, cols(h)]
        top = jnp.max(score.reshape(n // 8, 8, ROWS), axis=0)
        new = jnp.maximum(old, jnp.max(top, axis=0, keepdims=True))
        w = jnp.exp2(score - new[:1])
        if visible is not None:
            w = jnp.where(visible, w, 0.0)
        alpha = jnp.exp2(old - new)
        ml_ref[s, 8:, cols(h)] = ml_ref[s, 8:, cols(h)] * alpha + jnp.sum(w.reshape(n // 8, 8, ROWS), axis=0)
        p_refs[slot][:n] = w.astype(BF16)
        al_refs[slot][...] = alpha
        ml_ref[s, :8, cols(h)] = new

    def gather(s, v, h, slot):
        acc[s, :, cols(h)] = acc[s, :, cols(h)] * al_refs[slot][:1] + dot(v, p_refs[slot][: v.shape[1]])

    def tiles(list_of, visible=None, after_set=None):
        s, h, k, v = list_of[0]
        scores(s, k, h, 0)
        for n, (s, h, k, v) in enumerate(list_of):
            if n + 1 < len(list_of):
                s_next, h_next, k_next, _ = list_of[n + 1]
                scores(s_next, k_next, h_next, (n + 1) % 2)
            if n > 0:
                s_last, h_last, _, v_last = list_of[n - 1]
                gather(s_last, v_last, h_last, (n - 1) % 2)
            weigh(s, h, n % 2, k.shape[0], visible)
            if n == HEADS and after_set is not None:
                after_set()
        s, h, k, v = list_of[-1]
        gather(s, v, h, (len(list_of) - 1) % 2)

    def own_block():
        key_at = lax.broadcasted_iota(jnp.int32, (ROWS, ROWS), 0)
        query_at = lax.broadcasted_iota(jnp.int32, (ROWS, ROWS), 1)
        k = blocks[place, :ROWS]
        k = jnp.concatenate([k, k], 1)
        v = jnp.concatenate([blocks[place, ROWS : ROWS + HD], blocks[place, ROWS + HD :]], 1)
        tiles([(0, h, k, v) for h in range(HEADS)], key_at <= query_at)

    def own_plane(s):
        set_at = jnp.where(s < 2, y, 1 - y) * 2 + jnp.where(s % 2 == 0, core, 1 - core)
        seen = x + jnp.where(set_at > y * 2 + core, 1, 0)
        for count in (1, 2, 3, 4):
            @pl.when(seen == count)
            def _(count=count):
                k, v = keys(z, count), values(z, count)
                tiles([(s, h, k, v) for h in range(HEADS)])

    def relay(step_up, step_across):
        @pl.when(core == 0)
        def _():
            for dx in (1, 3, 2):
                mate = (x + dx) % 4

                @pl.when(jnp.logical_or(through, mate < x))
                def _(mate=mate):
                    step_up(mate)

        @pl.when(core == 1)
        def _():
            for dz in (1, 2, 3):
                @pl.when(z >= dz)
                def _(dz=dz):
                    step_across(z - dz)

    def relay_up(mate):
        wait_block(z * 4 + mate)
        up(mate, start)

    def relay_across(plane):
        wait_block(plane * 4 + x)
        across(plane, start)

    def plane_at(t):
        plane = z - 1 - t
        return jnp.where(jnp.logical_and(z == 3, plane < 2), 1 - plane, plane)

    def arrive(plane):
        for column in range(4):
            @pl.when(jnp.logical_or(along_x, x != column))
            def _(column=column):
                wait_block(plane * 4 + column)

    def hand_over(s, slot):
        return (
            copy(acc.at[s], got_acc.at[slot], acc_send.at[slot], acc_recv.at[slot], sibling),
            copy(ml_ref.at[s], got_ml.at[slot], stat_send.at[slot], stat_recv.at[slot], sibling),
        )

    def merged(s, slot):
        m, l = ml_ref[s, 0:1], jnp.sum(ml_ref[s, 8:], axis=0, keepdims=True)
        m_got, l_got = got_ml[slot, 0:1], jnp.sum(got_ml[slot, 8:], axis=0, keepdims=True)
        top = jnp.maximum(m, m_got)
        f, f_got = jnp.exp2(m - top), jnp.exp2(m_got - top)
        total = l * f + l_got * f_got
        return top, total, f, f_got

    ready_queries(0)
    own_block()
    relay(relay_up, relay_across)

    @pl.when(core == 1)
    def _():
        for column in range(3):
            @pl.when(column < x)
            def _(column=column):
                wait_block(z * 4 + column)

    def plane_step(s, _):
        @pl.when(s == 1)
        def _():
            q_to_sibling.wait_recv()

        @pl.when(s == 2)
        def _():
            q_to_partner.wait_recv()
            q_passed.start()

        @pl.when(s == 3)
        def _():
            q_passed.wait_recv()

        @pl.when(s > 0)
        def _():
            ready_queries(s)

        own_plane(s)
        return 0

    lax.fori_loop(0, SETS, plane_step, 0)

    def give():
        for c in hand_over(3, 0):
            c.start()

    @pl.when(z == 0)
    def _():
        give()

    def other_layer(t, _):
        plane = plane_at(t)
        arrive(plane)
        k, v = keys(plane, 4), values(plane, 4)

        def done():
            @pl.when(t == z - 1)
            def _():
                give()

        tiles([(s, h, k, v) for s in (3, 2) for h in range(HEADS)], after_set=done)
        return 0

    lax.fori_loop(0, z, other_layer, 0)

    def own_layer(s, lo, hi):
        @pl.when(lo < hi)
        def _():
            scores(s, keys(plane_at(lo), 4), 0, 0)
            p_b[...] = jnp.zeros(p_b.shape, BF16)
            al_b[...] = jnp.ones(al_b.shape, F32)

            def step(t, _):
                k, v = keys(plane_at(t), 4), values(plane_at(t), 4)
                k_next = keys(plane_at(jnp.minimum(t + 1, hi - 1)), 4)
                v_last = values(plane_at(jnp.maximum(t - 1, lo)), 4)
                for h in range(HEADS):
                    if h + 1 < HEADS:
                        scores(s, k, h + 1, (h + 1) % 2)
                    else:
                        scores(s, k_next, 0, 0)
                    if h > 0:
                        gather(s, v, h - 1, (h - 1) % 2)
                    else:
                        gather(s, v_last, HEADS - 1, 1)
                    weigh(s, h, h % 2, KEYS, None)
                return 0

            lax.fori_loop(lo, hi, step, 0)
            gather(s, values(plane_at(hi - 1), 4), HEADS - 1, 1)

    first = jnp.minimum(z, 1)
    own_layer(1, 0, first)

    for c in hand_over(3, 0):
        c.wait_recv()
    top, total, f, f_got = merged(2, 0)
    part_ml[0:1] = top
    part_ml[1:2] = total
    part_ml[2:] = jnp.zeros((6, COLS), F32)
    safe = 1.0 / jnp.where(total > 0, total, 1.0)
    part_o[...] = (acc[2] * (f * safe) + got_acc[0] * (f_got * safe)).astype(BF16)
    o_copy = copy(part_o, got_o, o_sem.at[0], o_sem.at[1], partner)
    oml_copy = copy(part_ml, got_oml, oml_sem.at[0], oml_sem.at[1], partner)
    o_copy.start()
    oml_copy.start()

    own_layer(1, first, z)
    for c in hand_over(1, 1):
        c.start()
    own_layer(0, 0, z)

    for c in hand_over(1, 1):
        c.wait_recv()
    m_own, total, f, f_got = merged(0, 1)
    o_copy.wait_recv()
    oml_copy.wait_recv()
    m_got = got_oml[0:1]
    top = jnp.maximum(m_own, m_got)
    a_own = jnp.exp2(m_own - top)
    a_got = jnp.exp2(m_got - top) * got_oml[1:2]
    inv = 1.0 / (total * a_own + a_got)
    f, f_got, f_far = f * (a_own * inv), f_got * (a_own * inv), a_got * inv
    for h in range(HEADS):
        o = acc[0, :, cols(h)] * f[:, cols(h)] + got_acc[1, :, cols(h)] * f_got[:, cols(h)]
        o = o + got_o[:, cols(h)].astype(F32) * f_far[:, cols(h)]
        out_ref[:, h * HD : (h + 1) * HD] = jnp.transpose(o).astype(BF16)

    for c in (q_to_sibling, q_to_partner, q_passed, o_copy, oml_copy) + hand_over(3, 0) + hand_over(1, 1):
        c.wait_send()
    own_across(gone)
    up(x, gone)
    relay(lambda mate: up(mate, gone), lambda plane: across(plane, gone))


def per_device(queries, key_rows, value_rows):
    return pl.pallas_call(
        kernel,
        out_shape=jax.ShapeDtypeStruct((ROWS, HEADS * HD), BF16),
        in_specs=[pl.BlockSpec(memory_space=pl.ANY)] * 3,
        out_specs=pl.BlockSpec(memory_space=pltpu.VMEM),
        scratch_shapes=[
            pltpu.VMEM((PLACES, 2 * ROWS, HD), BF16),
            pltpu.VMEM((ROWS, HD), BF16),
            pltpu.VMEM((SETS, ROWS, HEADS * HD), BF16),
            pltpu.VMEM((SETS, 2 * HD, COLS), BF16),
            pltpu.VMEM((SETS, 16, COLS), F32),
            pltpu.VMEM((SETS, HD, COLS), F32),
            pltpu.VMEM((KEYS, ROWS), F32),
            pltpu.VMEM((KEYS, ROWS), F32),
            pltpu.VMEM((KEYS, ROWS), BF16),
            pltpu.VMEM((KEYS, ROWS), BF16),
            pltpu.VMEM((8, ROWS), F32),
            pltpu.VMEM((8, ROWS), F32),
            pltpu.VMEM((2, HD, COLS), F32),
            pltpu.VMEM((2, 16, COLS), F32),
            pltpu.VMEM((HD, COLS), BF16),
            pltpu.VMEM((8, COLS), F32),
            pltpu.VMEM((HD, COLS), BF16),
            pltpu.VMEM((8, COLS), F32),
            pltpu.SemaphoreType.DMA((3,)),
            pltpu.SemaphoreType.DMA((4, 4)),
            pltpu.SemaphoreType.DMA((4, 4)),
            pltpu.SemaphoreType.DMA((PLACES,)),
            pltpu.SemaphoreType.DMA((3,)),
            pltpu.SemaphoreType.DMA((3,)),
            pltpu.SemaphoreType.DMA((2,)),
            pltpu.SemaphoreType.DMA((2,)),
            pltpu.SemaphoreType.DMA((2,)),
            pltpu.SemaphoreType.DMA((2,)),
            pltpu.SemaphoreType.DMA((2,)),
            pltpu.SemaphoreType.DMA((2,)),
        ],
        compiler_params=pltpu.CompilerParams(
            collective_id=0, has_side_effects=True, vmem_limit_bytes=60 << 20
        ),
        name="attend",
    )(queries, key_rows, value_rows)


def solution(mesh):
    placed = (P("ctx", "grp"), P("ctx", "grp"), P("ctx", "grp"))
    return jax.shard_map(
        per_device, mesh=mesh, in_specs=placed, out_specs=P("ctx", "grp"), check_vma=False
    )
```

time: 47.4 us -> 43 us (0.907)
  the two profiles are of different devices: /device:TPU:70 before, /device:TPU:102 now
where the time goes in v3:
time: 43 us; the launch traced here: 42.9 us
  Pallas kernels  41.2 us (96%)
  local copies, waits for them, and re-layouts  1.67 us (4%)
    pallas_call x1, Pallas kernels, per_device(): pl.pallas_call(kernel, out_shape=jax.ShapeDtypeStruct((ROWS, HEADS * HD),...  41.2 us
    unnamed x1, local copies, waits for them, and re-layouts  1.67 us

profile of v3, /device:TPU:102, one launch (start us, length us, event | category | flops | bytes accessed | tf_op | source)
XLA Modules:
  0.0 42.9 jit_solution(5339171265399251553)
XLA Ops:
  0.0 41.2 %attend.1 = bf16[256,512]{1,0:T(8,128)(2,1)} custom-call(bf16[256,512]{1,0:T(8,128)(2,1)} %q_in.1, bf16[256,128]{1,0:T(8,128)(2,1)} %k_in.1, bf16[256,128]{1,0:T(8,128)(2,1)} %v_in.1), custom_call_target="tpu_custom_call" | custom-call | tf_op jit(solution)/shard_map/attend/pallas_call | solution.py:403
  41.2 1.7 %copy.5 = bf16[256,512]{1,0:T(8,128)(2,1)} copy(bf16[256,512]{1,0:T(8,128)(2,1)} %attend.1) | data formatting | bytes 524288

commit v4 on v3

--- a/solution.py
+++ b/solution.py
@@ -18,6 +18,8 @@
 PLACES = 16
 KEYS = 4 * ROWS
 SETS = 4
+HELP = 4
+EXTRA = 3
 
 
 def dot(a, b):
@@ -27,8 +29,9 @@
 def kernel(
     q_in, k_in, v_in, out_ref,
     blocks, v_own, q_sets, q_t, ml_ref, acc, s_a, s_b, p_a, p_b, al_a, al_b,
-    got_acc, got_ml, part_o, part_ml, got_o, got_oml,
+    got_acc, got_ml, part_o, part_ml, got_o, got_oml, part_h, part_hml, got_h, got_hml,
     in_sem, x_sem, z_sem, from_sem, q_send, q_recv, acc_send, acc_recv, stat_send, stat_recv, o_sem, oml_sem,
+    share_send, qh_sem, h_sem, hml_sem,
 ):
     ctx = lax.axis_index("ctx")
     grp = lax.axis_index("grp")
@@ -43,7 +46,9 @@
     def at(other_place):
         return (other_place * 4 + y * 2 + core, grp)
 
-    through = jnp.where(along_x, z < 3, z > 0)
+    through = jnp.logical_or(jnp.logical_not(along_x), z < 3)
+    helped = at(12 + x)
+    helper = at(x)
 
     def mates(step):
         for dx in (1, 3, 2):
@@ -72,9 +77,18 @@
         def _(below=below):
             pl.semaphore_signal(barrier, inc=1, device_id=at(below * 4 + x), device_id_type=MESH)
 
-    ml_ref[:, :8] = jnp.full((SETS, 8, COLS), LOW, F32)
-    ml_ref[:, 8:] = jnp.zeros((SETS, 8, COLS), F32)
+    @pl.when(z == 0)
+    def _():
+        pl.semaphore_signal(barrier, inc=1, device_id=helped, device_id_type=MESH)
+
+    ml_ref[:, :8] = jnp.full((SETS + 1, 8, COLS), LOW, F32)
+    ml_ref[:, 8:] = jnp.zeros((SETS + 1, 8, COLS), F32)
     acc[...] = jnp.zeros(acc.shape, F32)
+
+    @pl.when(z != 3)
+    def _():
+        got_h[...] = jnp.zeros(got_h.shape, BF16)
+        got_hml[...] = jnp.full(got_hml.shape, LOW, F32)
 
     v_get.wait()
     v_t = jnp.transpose(v_own[...].astype(F32)).astype(BF16)
@@ -83,7 +97,7 @@
     k_get.wait()
     q_get.wait()
 
-    pl.semaphore_wait(barrier, 5 - z + jnp.where(through, 3, 3 - x))
+    pl.semaphore_wait(barrier, 5 - z + jnp.where(z == 3, 1, 0) + jnp.where(through, 3, 3 - x))
 
     def copy(src, dst, send, recv, device):
         return pltpu.make_async_remote_copy(
@@ -103,7 +117,7 @@
         copy(blocks.at[here], blocks.at[here], x_sem.at[0, 0], from_sem.at[here], sibling).wait_recv()
 
     def up(column, step):
-        for dz in (1, 2, 3):
+        for dz in (1, 2):
             @pl.when(z + dz < 4)
             def _(dz=dz):
                 step(along_z_copy(column, z + dz))
@@ -116,10 +130,27 @@
         for dx in (1, 3, 2):
             mate = (x + dx) % 4
 
-            @pl.when(jnp.logical_or(jnp.logical_and(along_x, z < 3), mate > x))
+            @pl.when(jnp.logical_or(jnp.logical_or(jnp.logical_and(along_x, z < 3), z == 0), mate > x))
             def _(mate=mate):
                 step(along_x_copy(z, mate))
 
+    def share_copies(column):
+        return (
+            copy(blocks.at[column], blocks.at[16 + column], share_send.at[0, column], from_sem.at[16 + column], sibling),
+            copy(blocks.at[column], blocks.at[20 + column], share_send.at[1, column], from_sem.at[20 + column], partner),
+        )
+
+    def share_pass(column):
+        return copy(
+            blocks.at[20 + column], blocks.at[24 + column], share_send.at[2, column], from_sem.at[24 + column], sibling
+        )
+
+    def share(column):
+        @pl.when(z == 0)
+        def _():
+            for c in share_copies(column):
+                c.start()
+
     def start(c):
         c.start()
 
@@ -128,10 +159,16 @@
 
     q_to_sibling = copy(q_sets.at[0], q_sets.at[1], q_send.at[0], q_recv.at[0], sibling)
     q_to_partner = copy(q_sets.at[0], q_sets.at[2], q_send.at[1], q_recv.at[1], partner)
+    q_help = copy(q_sets.at[0], q_sets.at[HELP], qh_sem.at[0], qh_sem.at[1], helper)
+    h_copy = copy(part_h, got_h, h_sem.at[0], h_sem.at[1], helped)
+    hml_copy = copy(part_hml, got_hml, hml_sem.at[0], hml_sem.at[1], helped)
     q_passed = copy(q_sets.at[2], q_sets.at[3], q_send.at[2], q_recv.at[2], sibling)
 
-    q_to_partner.start()
     q_to_sibling.start()
+
+    @pl.when(z == 3)
+    def _():
+        q_help.start()
 
     @pl.when(core == 0)
     def _():
@@ -142,6 +179,9 @@
     def _():
         up(x, start)
         own_across(start)
+
+    q_to_partner.start()
+    share(x)
 
     scale = math.log2(math.e) / math.sqrt(HD)
 
@@ -235,7 +275,7 @@
 
         @pl.when(core == 1)
         def _():
-            for dz in (1, 2, 3):
+            for dz in (1, 2):
                 @pl.when(z >= dz)
                 def _(dz=dz):
                     step_across(z - dz)
@@ -243,14 +283,14 @@
     def relay_up(mate):
         wait_block(z * 4 + mate)
         up(mate, start)
+        share(mate)
 
     def relay_across(plane):
         wait_block(plane * 4 + x)
         across(plane, start)
 
     def plane_at(t):
-        plane = z - 1 - t
-        return jnp.where(jnp.logical_and(z == 3, plane < 2), 1 - plane, plane)
+        return z - 1 - t
 
     def arrive(plane):
         for column in range(4):
@@ -278,10 +318,11 @@
 
     @pl.when(core == 1)
     def _():
-        for column in range(3):
-            @pl.when(column < x)
+        for column in range(4):
+            @pl.when(jnp.logical_or(jnp.logical_and(z == 0, column != x), column < x))
             def _(column=column):
                 wait_block(z * 4 + column)
+                share(column)
 
     def plane_step(s, _):
         @pl.when(s == 1)
@@ -320,16 +361,17 @@
         k, v = keys(plane, 4), values(plane, 4)
 
         def done():
-            @pl.when(t == z - 1)
+            @pl.when(t == planes - 1)
             def _():
                 give()
 
         tiles([(s, h, k, v) for s in (3, 2) for h in range(HEADS)], after_set=done)
         return 0
 
-    lax.fori_loop(0, z, other_layer, 0)
-
-    def own_layer(s, lo, hi):
+    planes = jnp.minimum(z, 2)
+    lax.fori_loop(0, planes, other_layer, 0)
+
+    def own_layer(s, lo, hi, plane_at=plane_at):
         @pl.when(lo < hi)
         def _():
             scores(s, keys(plane_at(lo), 4), 0, 0)
@@ -355,7 +397,18 @@
             lax.fori_loop(lo, hi, step, 0)
             gather(s, values(plane_at(hi - 1), 4), HEADS - 1, 1)
 
-    first = jnp.minimum(z, 1)
+    def help_at(t):
+        return jnp.where(t == 0, 0, t + 3)
+
+    @pl.when(z == 0)
+    def _():
+        q_help.wait_recv()
+        ready_queries(HELP)
+        for column in range(4):
+            wait_block(16 + column)
+        own_layer(HELP, 0, 2, help_at)
+
+    first = jnp.minimum(planes, 1)
     own_layer(1, 0, first)
 
     for c in hand_over(3, 0):
@@ -371,31 +424,68 @@
     o_copy.start()
     oml_copy.start()
 
-    own_layer(1, first, z)
+    own_layer(1, first, planes)
     for c in hand_over(1, 1):
         c.start()
-    own_layer(0, 0, z)
+    own_layer(0, 0, planes)
+
+    @pl.when(z == 0)
+    def _():
+        for column in range(4):
+            wait_block(20 + column)
+            share_pass(column).start()
+        own_layer(HELP, 2, 3, help_at)
+        for column in range(4):
+            wait_block(24 + column)
+        own_layer(HELP, 3, 4, help_at)
+        l_h = jnp.sum(ml_ref[HELP, 8:], axis=0, keepdims=True)
+        part_hml[0:1] = ml_ref[HELP, 0:1]
+        part_hml[1:2] = l_h
+        part_hml[2:] = jnp.zeros((6, COLS), F32)
+        part_h[...] = (acc[HELP] * (1.0 / l_h)).astype(BF16)
+        h_copy.start()
+        hml_copy.start()
 
     for c in hand_over(1, 1):
         c.wait_recv()
     m_own, total, f, f_got = merged(0, 1)
     o_copy.wait_recv()
     oml_copy.wait_recv()
-    m_got = got_oml[0:1]
-    top = jnp.maximum(m_own, m_got)
+
+    @pl.when(z == 3)
+    def _():
+        h_copy.wait_recv()
+        hml_copy.wait_recv()
+
+    m_got, m_h = got_oml[0:1], got_hml[0:1]
+    top = jnp.maximum(jnp.maximum(m_own, m_got), m_h)
     a_own = jnp.exp2(m_own - top)
     a_got = jnp.exp2(m_got - top) * got_oml[1:2]
-    inv = 1.0 / (total * a_own + a_got)
-    f, f_got, f_far = f * (a_own * inv), f_got * (a_own * inv), a_got * inv
+    a_h = jnp.where(z == 3, jnp.exp2(m_h - top) * got_hml[1:2], 0.0)
+    inv = 1.0 / (total * a_own + a_got + a_h)
+    f, f_got, f_far, f_h = f * (a_own * inv), f_got * (a_own * inv), a_got * inv, a_h * inv
     for h in range(HEADS):
         o = acc[0, :, cols(h)] * f[:, cols(h)] + got_acc[1, :, cols(h)] * f_got[:, cols(h)]
-        o = o + got_o[:, cols(h)].astype(F32) * f_far[:, cols(h)]
+        o = o + got_o[:, cols(h)].astype(F32) * f_far[:, cols(h)] + got_h[:, cols(h)].astype(F32) * f_h[:, cols(h)]
         out_ref[:, h * HD : (h + 1) * HD] = jnp.transpose(o).astype(BF16)
 
     for c in (q_to_sibling, q_to_partner, q_passed, o_copy, oml_copy) + hand_over(3, 0) + hand_over(1, 1):
         c.wait_send()
     own_across(gone)
     up(x, gone)
+
+    @pl.when(z == 3)
+    def _():
+        q_help.wait_send()
+
+    @pl.when(z == 0)
+    def _():
+        h_copy.wait_send()
+        hml_copy.wait_send()
+        for column in range(4):
+            for c in share_copies(column) + (share_pass(column),):
+                c.wait_send()
+
     relay(lambda mate: up(mate, gone), lambda plane: across(plane, gone))
 
 
@@ -406,12 +496,12 @@
         in_specs=[pl.BlockSpec(memory_space=pl.ANY)] * 3,
         out_specs=pl.BlockSpec(memory_space=pltpu.VMEM),
         scratch_shapes=[
-            pltpu.VMEM((PLACES, 2 * ROWS, HD), BF16),
+            pltpu.VMEM((PLACES + 4 * EXTRA, 2 * ROWS, HD), BF16),
             pltpu.VMEM((ROWS, HD), BF16),
-            pltpu.VMEM((SETS, ROWS, HEADS * HD), BF16),
-            pltpu.VMEM((SETS, 2 * HD, COLS), BF16),
-            pltpu.VMEM((SETS, 16, COLS), F32),
-            pltpu.VMEM((SETS, HD, COLS), F32),
+            pltpu.VMEM((SETS + 1, ROWS, HEADS * HD), BF16),
+            pltpu.VMEM((SETS + 1, 2 * HD, COLS), BF16),
+            pltpu.VMEM((SETS + 1, 16, COLS), F32),
+            pltpu.VMEM((SETS + 1, HD, COLS), F32),
             pltpu.VMEM((KEYS, ROWS), F32),
             pltpu.VMEM((KEYS, ROWS), F32),
             pltpu.VMEM((KEYS, ROWS), BF16),
@@ -424,15 +514,23 @@
             pltpu.VMEM((8, COLS), F32),
             pltpu.VMEM((HD, COLS), BF16),
             pltpu.VMEM((8, COLS), F32),
+            pltpu.VMEM((HD, COLS), BF16),
+            pltpu.VMEM((8, COLS), F32),
+            pltpu.VMEM((HD, COLS), BF16),
+            pltpu.VMEM((8, COLS), F32),
             pltpu.SemaphoreType.DMA((3,)),
             pltpu.SemaphoreType.DMA((4, 4)),
             pltpu.SemaphoreType.DMA((4, 4)),
-            pltpu.SemaphoreType.DMA((PLACES,)),
+            pltpu.SemaphoreType.DMA((PLACES + 4 * EXTRA,)),
             pltpu.SemaphoreType.DMA((3,)),
             pltpu.SemaphoreType.DMA((3,)),
             pltpu.SemaphoreType.DMA((2,)),
             pltpu.SemaphoreType.DMA((2,)),
             pltpu.SemaphoreType.DMA((2,)),
+            pltpu.SemaphoreType.DMA((2,)),
+            pltpu.SemaphoreType.DMA((2,)),
+            pltpu.SemaphoreType.DMA((2,)),
+            pltpu.SemaphoreType.DMA((3, 4)),
             pltpu.SemaphoreType.DMA((2,)),
             pltpu.SemaphoreType.DMA((2,)),
             pltpu.SemaphoreType.DMA((2,)),

time: 43 us -> 40.9 us (0.951)
  the two profiles are of different devices: /device:TPU:102 before, /device:TPU:70 now
where the time goes in v4:
time: 40.9 us; the launch traced here: 40.7 us
  Pallas kernels  39 us (95%)
  local copies, waits for them, and re-layouts  1.67 us (4%)
    pallas_call x1, Pallas kernels, per_device(): pl.pallas_call(kernel, out_shape=jax.ShapeDtypeStruct((ROWS, HEADS * HD),...  39 us
    unnamed x1, local copies, waits for them, and re-layouts  1.67 us

profile of v4, /device:TPU:70, one launch (start us, length us, event | category | flops | bytes accessed | tf_op | source)
XLA Modules:
  0.0 40.7 jit_solution(6201473284683528225)
XLA Ops:
  0.0 39.0 %attend.1 = bf16[256,512]{1,0:T(8,128)(2,1)} custom-call(bf16[256,512]{1,0:T(8,128)(2,1)} %q_in.1, bf16[256,128]{1,0:T(8,128)(2,1)} %k_in.1, bf16[256,128]{1,0:T(8,128)(2,1)} %v_in.1), custom_call_target="tpu_custom_call" | custom-call | tf_op jit(solution)/shard_map/attend/pallas_call | solution.py:493
  39.0 1.7 %copy.5 = bf16[256,512]{1,0:T(8,128)(2,1)} copy(bf16[256,512]{1,0:T(8,128)(2,1)} %attend.1) | data formatting | bytes 524288

commit v5 on v4

--- a/solution.py
+++ b/solution.py
@@ -166,21 +166,28 @@
 
     q_to_sibling.start()
 
+    @pl.when(core == 0)
+    def _():
+        own_across(start)
+
+    @pl.when(core == 1)
+    def _():
+        up(x, start)
+
+    q_to_partner.start()
+
+    @pl.when(core == 0)
+    def _():
+        up(x, start)
+
+    @pl.when(core == 1)
+    def _():
+        own_across(start)
+
     @pl.when(z == 3)
     def _():
         q_help.start()
 
-    @pl.when(core == 0)
-    def _():
-        own_across(start)
-        up(x, start)
-
-    @pl.when(core == 1)
-    def _():
-        up(x, start)
-        own_across(start)
-
-    q_to_partner.start()
     share(x)
 
     scale = math.log2(math.e) / math.sqrt(HD)
@@ -230,7 +237,7 @@
     def gather(s, v, h, slot):
         acc[s, :, cols(h)] = acc[s, :, cols(h)] * al_refs[slot][:1] + dot(v, p_refs[slot][: v.shape[1]])
 
-    def tiles(list_of, visible=None, after_set=None):
+    def tiles(list_of, visible=None):
         s, h, k, v = list_of[0]
         scores(s, k, h, 0)
         for n, (s, h, k, v) in enumerate(list_of):
@@ -241,8 +248,6 @@
                 s_last, h_last, _, v_last = list_of[n - 1]
                 gather(s_last, v_last, h_last, (n - 1) % 2)
             weigh(s, h, n % 2, k.shape[0], visible)
-            if n == HEADS and after_set is not None:
-                after_set()
         s, h, k, v = list_of[-1]
         gather(s, v, h, (len(list_of) - 1) % 2)
 
@@ -314,6 +319,8 @@
 
     ready_queries(0)
     own_block()
+    q_to_sibling.wait_recv()
+    ready_queries(1)
     relay(relay_up, relay_across)
 
     @pl.when(core == 1)
@@ -324,10 +331,8 @@
                 wait_block(z * 4 + column)
                 share(column)
 
-    def plane_step(s, _):
-        @pl.when(s == 1)
-        def _():
-            q_to_sibling.wait_recv()
+    def plane_step(t, _):
+        s = t + 1
 
         @pl.when(s == 2)
         def _():
@@ -338,40 +343,16 @@
         def _():
             q_passed.wait_recv()
 
-        @pl.when(s > 0)
+        @pl.when(s > 1)
         def _():
             ready_queries(s)
 
         own_plane(s)
         return 0
 
-    lax.fori_loop(0, SETS, plane_step, 0)
-
-    def give():
-        for c in hand_over(3, 0):
-            c.start()
-
-    @pl.when(z == 0)
-    def _():
-        give()
-
-    def other_layer(t, _):
-        plane = plane_at(t)
-        arrive(plane)
-        k, v = keys(plane, 4), values(plane, 4)
-
-        def done():
-            @pl.when(t == planes - 1)
-            def _():
-                give()
-
-        tiles([(s, h, k, v) for s in (3, 2) for h in range(HEADS)], after_set=done)
-        return 0
-
-    planes = jnp.minimum(z, 2)
-    lax.fori_loop(0, planes, other_layer, 0)
-
-    def own_layer(s, lo, hi, plane_at=plane_at):
+    lax.fori_loop(0, 3, plane_step, 0)
+
+    def layers(s, lo, hi, plane_at=plane_at):
         @pl.when(lo < hi)
         def _():
             scores(s, keys(plane_at(lo), 4), 0, 0)
@@ -397,6 +378,20 @@
             lax.fori_loop(lo, hi, step, 0)
             gather(s, values(plane_at(hi - 1), 4), HEADS - 1, 1)
 
+    planes = jnp.minimum(z, 2)
+
+    def siblings_partner(t, _):
+        plane = plane_at(t)
+        arrive(plane)
+        k, v = keys(plane, 4), values(plane, 4)
+        tiles([(3, h, k, v) for h in range(HEADS)])
+        return 0
+
+    lax.fori_loop(0, planes, siblings_partner, 0)
+    for c in hand_over(3, 0):
+        c.start()
+    layers(2, 0, planes)
+
     def help_at(t):
         return jnp.where(t == 0, 0, t + 3)
 
@@ -406,10 +401,8 @@
         ready_queries(HELP)
         for column in range(4):
             wait_block(16 + column)
-        own_layer(HELP, 0, 2, help_at)
-
-    first = jnp.minimum(planes, 1)
-    own_layer(1, 0, first)
+        layers(HELP, 0, 2, help_at)
+
 
     for c in hand_over(3, 0):
         c.wait_recv()
@@ -424,20 +417,21 @@
     o_copy.start()
     oml_copy.start()
 
-    own_layer(1, first, planes)
+    layers(1, 0, planes)
     for c in hand_over(1, 1):
         c.start()
-    own_layer(0, 0, planes)
+    own_plane(0)
+    layers(0, 0, planes)
 
     @pl.when(z == 0)
     def _():
         for column in range(4):
             wait_block(20 + column)
             share_pass(column).start()
-        own_layer(HELP, 2, 3, help_at)
+        layers(HELP, 2, 3, help_at)
         for column in range(4):
             wait_block(24 + column)
-        own_layer(HELP, 3, 4, help_at)
+        layers(HELP, 3, 4, help_at)
         l_h = jnp.sum(ml_ref[HELP, 8:], axis=0, keepdims=True)
         part_hml[0:1] = ml_ref[HELP, 0:1]
         part_hml[1:2] = l_h

time: 40.9 us -> 39.5 us (0.966)
  Pallas kernels: 39 us -> 37.4 us
    pallas_call x1, Pallas kernels: 39 us -> 37.4 us  [per_device(): pl.pallas_call(kernel, out_shape=jax.ShapeDtypeStruct((ROWS, HEADS * HD),...]
where the time goes in v5:
time: 39.5 us; the launch traced here: 39.1 us
  Pallas kernels  37.4 us (95%)
  local copies, waits for them, and re-layouts  1.67 us (4%)
    pallas_call x1, Pallas kernels, per_device(): pl.pallas_call(kernel, out_shape=jax.ShapeDtypeStruct((ROWS, HEADS * HD),...  37.4 us
    unnamed x1, local copies, waits for them, and re-layouts  1.67 us

profile of v5, /device:TPU:70, one launch (start us, length us, event | category | flops | bytes accessed | tf_op | source)
XLA Modules:
  0.0 39.1 jit_solution(13022495744851245419)
XLA Ops:
  0.0 37.4 %attend.1 = bf16[256,512]{1,0:T(8,128)(2,1)} custom-call(bf16[256,512]{1,0:T(8,128)(2,1)} %q_in.1, bf16[256,128]{1,0:T(8,128)(2,1)} %k_in.1, bf16[256,128]{1,0:T(8,128)(2,1)} %v_in.1), custom_call_target="tpu_custom_call" | custom-call | tf_op jit(solution)/shard_map/attend/pallas_call | solution.py:487
  37.4 1.7 %copy.5 = bf16[256,512]{1,0:T(8,128)(2,1)} copy(bf16[256,512]{1,0:T(8,128)(2,1)} %attend.1) | data formatting | bytes 524288

commit v6 on v5

--- a/solution.py
+++ b/solution.py
@@ -90,6 +90,15 @@
         got_h[...] = jnp.zeros(got_h.shape, BF16)
         got_hml[...] = jnp.full(got_hml.shape, LOW, F32)
 
+    @pl.when(z == 0)
+    def _():
+        got_acc[1] = jnp.zeros((HD, COLS), F32)
+        got_ml[1, :8] = jnp.full((8, COLS), LOW, F32)
+        got_ml[1, 8:] = jnp.zeros((8, COLS), F32)
+        got_o[...] = jnp.zeros(got_o.shape, BF16)
+        got_oml[0:1] = jnp.full((1, COLS), LOW, F32)
+        got_oml[1:] = jnp.zeros((7, COLS), F32)
+
     v_get.wait()
     v_t = jnp.transpose(v_own[...].astype(F32)).astype(BF16)
     blocks[place, ROWS : ROWS + HD] = v_t[:, :HD]
@@ -117,7 +126,7 @@
         copy(blocks.at[here], blocks.at[here], x_sem.at[0, 0], from_sem.at[here], sibling).wait_recv()
 
     def up(column, step):
-        for dz in (1, 2):
+        for dz in (2, 1):
             @pl.when(z + dz < 4)
             def _(dz=dz):
                 step(along_z_copy(column, z + dz))
@@ -164,7 +173,9 @@
     hml_copy = copy(part_hml, got_hml, hml_sem.at[0], hml_sem.at[1], helped)
     q_passed = copy(q_sets.at[2], q_sets.at[3], q_send.at[2], q_recv.at[2], sibling)
 
-    q_to_sibling.start()
+    @pl.when(z > 0)
+    def _():
+        q_to_sibling.start()
 
     @pl.when(core == 0)
     def _():
@@ -174,7 +185,9 @@
     def _():
         up(x, start)
 
-    q_to_partner.start()
+    @pl.when(z > 0)
+    def _():
+        q_to_partner.start()
 
     @pl.when(core == 0)
     def _():
@@ -262,10 +275,13 @@
     def own_plane(s):
         set_at = jnp.where(s < 2, y, 1 - y) * 2 + jnp.where(s % 2 == 0, core, 1 - core)
         seen = x + jnp.where(set_at > y * 2 + core, 1, 0)
+        first_places(s, z, seen)
+
+    def first_places(s, plane, seen):
         for count in (1, 2, 3, 4):
             @pl.when(seen == count)
             def _(count=count):
-                k, v = keys(z, count), values(z, count)
+                k, v = keys(plane, count), values(plane, count)
                 tiles([(s, h, k, v) for h in range(HEADS)])
 
     def relay(step_up, step_across):
@@ -319,8 +335,12 @@
 
     ready_queries(0)
     own_block()
-    q_to_sibling.wait_recv()
-    ready_queries(1)
+
+    @pl.when(z > 0)
+    def _():
+        q_to_sibling.wait_recv()
+        ready_queries(1)
+
     relay(relay_up, relay_across)
 
     @pl.when(core == 1)
@@ -350,7 +370,7 @@
         own_plane(s)
         return 0
 
-    lax.fori_loop(0, 3, plane_step, 0)
+    lax.fori_loop(0, jnp.where(z > 0, 3, 0), plane_step, 0)
 
     def layers(s, lo, hi, plane_at=plane_at):
         @pl.when(lo < hi)
@@ -388,8 +408,12 @@
         return 0
 
     lax.fori_loop(0, planes, siblings_partner, 0)
-    for c in hand_over(3, 0):
-        c.start()
+
+    @pl.when(z > 0)
+    def _():
+        for c in hand_over(3, 0):
+            c.start()
+
     layers(2, 0, planes)
 
     def help_at(t):
@@ -404,22 +428,35 @@
         layers(HELP, 0, 2, help_at)
 
 
-    for c in hand_over(3, 0):
-        c.wait_recv()
-    top, total, f, f_got = merged(2, 0)
-    part_ml[0:1] = top
-    part_ml[1:2] = total
-    part_ml[2:] = jnp.zeros((6, COLS), F32)
-    safe = 1.0 / jnp.where(total > 0, total, 1.0)
-    part_o[...] = (acc[2] * (f * safe) + got_acc[0] * (f_got * safe)).astype(BF16)
-    o_copy = copy(part_o, got_o, o_sem.at[0], o_sem.at[1], partner)
     oml_copy = copy(part_ml, got_oml, oml_sem.at[0], oml_sem.at[1], partner)
-    o_copy.start()
-    oml_copy.start()
+    halves = [slice(half * COLS // 2, (half + 1) * COLS // 2) for half in range(2)]
+    o_copies = [
+        copy(part_o.at[:, part], got_o.at[:, part], o_sem.at[0, half], o_sem.at[1, half], partner)
+        for half, part in enumerate(halves)
+    ]
+
+    @pl.when(z > 0)
+    def _():
+        for c in hand_over(3, 0):
+            c.wait_recv()
+        top, total, f, f_got = merged(2, 0)
+        part_ml[0:1] = top
+        part_ml[1:2] = total
+        part_ml[2:] = jnp.zeros((6, COLS), F32)
+        oml_copy.start()
+        safe = 1.0 / jnp.where(total > 0, total, 1.0)
+        f, f_got = f * safe, f_got * safe
+        for part, c in zip(halves, o_copies):
+            part_o[:, part] = (acc[2, :, part] * f[:, part] + got_acc[0, :, part] * f_got[:, part]).astype(BF16)
+            c.start()
 
     layers(1, 0, planes)
-    for c in hand_over(1, 1):
-        c.start()
+
+    @pl.when(z > 0)
+    def _():
+        for c in hand_over(1, 1):
+            c.start()
+
     own_plane(0)
     layers(0, 0, planes)
 
@@ -440,11 +477,19 @@
         h_copy.start()
         hml_copy.start()
 
-    for c in hand_over(1, 1):
-        c.wait_recv()
+        def other_blocks(e, _):
+            first_places(0, 4 + e, x + jnp.where(e == 0, core, y))
+            return 0
+
+        lax.fori_loop(0, EXTRA, other_blocks, 0)
+
+    @pl.when(z > 0)
+    def _():
+        for c in hand_over(1, 1):
+            c.wait_recv()
+        oml_copy.wait_recv()
+
     m_own, total, f, f_got = merged(0, 1)
-    o_copy.wait_recv()
-    oml_copy.wait_recv()
 
     @pl.when(z == 3)
     def _():
@@ -459,12 +504,20 @@
     inv = 1.0 / (total * a_own + a_got + a_h)
     f, f_got, f_far, f_h = f * (a_own * inv), f_got * (a_own * inv), a_got * inv, a_h * inv
     for h in range(HEADS):
+        if h % 2 == 0:
+            @pl.when(z > 0)
+            def _(h=h):
+                o_copies[h // 2].wait_recv()
+
         o = acc[0, :, cols(h)] * f[:, cols(h)] + got_acc[1, :, cols(h)] * f_got[:, cols(h)]
         o = o + got_o[:, cols(h)].astype(F32) * f_far[:, cols(h)] + got_h[:, cols(h)].astype(F32) * f_h[:, cols(h)]
         out_ref[:, h * HD : (h + 1) * HD] = jnp.transpose(o).astype(BF16)
 
-    for c in (q_to_sibling, q_to_partner, q_passed, o_copy, oml_copy) + hand_over(3, 0) + hand_over(1, 1):
-        c.wait_send()
+    @pl.when(z > 0)
+    def _():
+        for c in (q_to_sibling, q_to_partner, q_passed, oml_copy, *o_copies) + hand_over(3, 0) + hand_over(1, 1):
+            c.wait_send()
+
     own_across(gone)
     up(x, gone)
 
@@ -522,7 +575,7 @@
             pltpu.SemaphoreType.DMA((2,)),
             pltpu.SemaphoreType.DMA((2,)),
             pltpu.SemaphoreType.DMA((2,)),
-            pltpu.SemaphoreType.DMA((2,)),
+            pltpu.SemaphoreType.DMA((2, 2)),
             pltpu.SemaphoreType.DMA((2,)),
             pltpu.SemaphoreType.DMA((3, 4)),
             pltpu.SemaphoreType.DMA((2,)),

time: 39.5 us -> 37.8 us (0.957)
  Pallas kernels: 37.4 us -> 35.9 us
    pallas_call x1, Pallas kernels: 37.4 us -> 35.9 us  [per_device(): pl.pallas_call(kernel, out_shape=jax.ShapeDtypeStruct((ROWS, HEADS * HD),...]
where the time goes in v6:
time: 37.8 us; the launch traced here: 37.6 us
  Pallas kernels  35.9 us (95%)
  local copies, waits for them, and re-layouts  1.67 us (4%)
    pallas_call x1, Pallas kernels, per_device(): pl.pallas_call(kernel, out_shape=jax.ShapeDtypeStruct((ROWS, HEADS * HD),...  35.9 us
    unnamed x1, local copies, waits for them, and re-layouts  1.67 us

profile of v6, /device:TPU:70, one launch (start us, length us, event | category | flops | bytes accessed | tf_op | source)
XLA Modules:
  0.0 37.6 jit_solution(4392944294166170528)
XLA Ops:
  0.0 35.9 %attend.1 = bf16[256,512]{1,0:T(8,128)(2,1)} custom-call(bf16[256,512]{1,0:T(8,128)(2,1)} %q_in.1, bf16[256,128]{1,0:T(8,128)(2,1)} %k_in.1, bf16[256,128]{1,0:T(8,128)(2,1)} %v_in.1), custom_call_target="tpu_custom_call" | custom-call | tf_op jit(solution)/shard_map/attend/pallas_call | solution.py:540
  35.9 1.7 %copy.5 = bf16[256,512]{1,0:T(8,128)(2,1)} copy(bf16[256,512]{1,0:T(8,128)(2,1)} %attend.1) | data formatting | bytes 524288

commit v7 on v6

--- a/solution.py
+++ b/solution.py
@@ -31,7 +31,7 @@
     blocks, v_own, q_sets, q_t, ml_ref, acc, s_a, s_b, p_a, p_b, al_a, al_b,
     got_acc, got_ml, part_o, part_ml, got_o, got_oml, part_h, part_hml, got_h, got_hml,
     in_sem, x_sem, z_sem, from_sem, q_send, q_recv, acc_send, acc_recv, stat_send, stat_recv, o_sem, oml_sem,
-    share_send, qh_sem, h_sem, hml_sem,
+    share_send, qh_sem, h_sem, hml_sem, out_buf, out_sem,
 ):
     ctx = lax.axis_index("ctx")
     grp = lax.axis_index("grp")
@@ -160,6 +160,10 @@
             for c in share_copies(column):
                 c.start()
 
+    def put(h):
+        part = pl.ds(h * HD, HD)
+        return pltpu.make_async_copy(out_buf.at[:, part], out_ref.at[:, part], out_sem.at[h])
+
     def start(c):
         c.start()
 
@@ -175,6 +179,7 @@
 
     @pl.when(z > 0)
     def _():
+        q_to_partner.start()
         q_to_sibling.start()
 
     @pl.when(core == 0)
@@ -184,10 +189,6 @@
     @pl.when(core == 1)
     def _():
         up(x, start)
-
-    @pl.when(z > 0)
-    def _():
-        q_to_partner.start()
 
     @pl.when(core == 0)
     def _():
@@ -511,7 +512,11 @@
 
         o = acc[0, :, cols(h)] * f[:, cols(h)] + got_acc[1, :, cols(h)] * f_got[:, cols(h)]
         o = o + got_o[:, cols(h)].astype(F32) * f_far[:, cols(h)] + got_h[:, cols(h)].astype(F32) * f_h[:, cols(h)]
-        out_ref[:, h * HD : (h + 1) * HD] = jnp.transpose(o).astype(BF16)
+        out_buf[:, h * HD : (h + 1) * HD] = jnp.transpose(o).astype(BF16)
+        put(h).start()
+
+    for h in range(HEADS):
+        put(h).wait()
 
     @pl.when(z > 0)
     def _():
@@ -541,7 +546,7 @@
         kernel,
         out_shape=jax.ShapeDtypeStruct((ROWS, HEADS * HD), BF16),
         in_specs=[pl.BlockSpec(memory_space=pl.ANY)] * 3,
-        out_specs=pl.BlockSpec(memory_space=pltpu.VMEM),
+        out_specs=pl.BlockSpec(memory_space=pl.ANY),
         scratch_shapes=[
             pltpu.VMEM((PLACES + 4 * EXTRA, 2 * ROWS, HD), BF16),
             pltpu.VMEM((ROWS, HD), BF16),
@@ -581,6 +586,8 @@
             pltpu.SemaphoreType.DMA((2,)),
             pltpu.SemaphoreType.DMA((2,)),
             pltpu.SemaphoreType.DMA((2,)),
+            pltpu.VMEM((ROWS, HEADS * HD), BF16),
+            pltpu.SemaphoreType.DMA((HEADS,)),
         ],
         compiler_params=pltpu.CompilerParams(
             collective_id=0, has_side_effects=True, vmem_limit_bytes=60 << 20

time: 37.8 us -> 37.8 us (level)
  no operation moved by 1% of the time
where the time goes in v7:
time: 37.8 us; the launch traced here: 37.6 us
  Pallas kernels  35.9 us (95%)
  local copies, waits for them, and re-layouts  1.67 us (4%)
    pallas_call x1, Pallas kernels, per_device(): pl.pallas_call(kernel, out_shape=jax.ShapeDtypeStruct((ROWS, HEADS * HD),...  35.9 us
    unnamed x1, local copies, waits for them, and re-layouts  1.67 us

profile of v7, /device:TPU:70, one launch (start us, length us, event | category | flops | bytes accessed | tf_op | source)
XLA Modules:
  0.0 37.6 jit_solution(9500815227207085945)
XLA Ops:
  0.0 35.9 %attend.1 = bf16[256,512]{1,0:T(8,128)(2,1)} custom-call(bf16[256,512]{1,0:T(8,128)(2,1)} %q_in.1, bf16[256,128]{1,0:T(8,128)(2,1)} %k_in.1, bf16[256,128]{1,0:T(8,128)(2,1)} %v_in.1), custom_call_target="tpu_custom_call" | custom-call | tf_op jit(solution)/shard_map/attend/pallas_call | solution.py:545
  35.9 1.7 %copy.5 = bf16[256,512]{1,0:T(8,128)(2,1)} copy(bf16[256,512]{1,0:T(8,128)(2,1)} %attend.1) | data formatting | bytes 524288
